TPU v7x, 32 devices: a whole 2x2x4 slice. The times are simulated.
32 devices in a mesh: freq: 16 (over z, y, core), kpt: 2 (over x).
Axes of the slice: x: 2, y: 2, z: 4, core: 2. Of those that a mesh axis runs over, the one named last changes fastest.
Arguments:
- band_energy: float32 [2, 384], P('kpt'), may hold values from -4.5 to 4.5, as said below
- projector: bfloat16 [2, 640, 384], P('kpt', 'freq'), may hold values from -0.25 to 0.25
- sigma: float32 [2, 5, 5, 128, 16], P(None, None, None, 'freq'), may hold values from -8.5 to 8.5, as said below
- atom_of_slot: int32 [128], replicated, may hold values from 0 to 127, each once
- kweight: int32 [2], replicated, may hold values from 1 to 16
Outputs:
- local_green: float32 [2, 5, 5, 128, 16], P(None, None, None, ('freq', 'kpt'))
Inputs may be any that keep to these rules, and one draw needn't show every extreme that they name: `band_energy`: every entry is a band energy; the energies of one k-point share a common offset drawn per k-point. Each block sigma[0, :, :, s, n] is symmetric; each block sigma[1, :, :, s, n] is symmetric and negative definite. `atom_of_slot`: A permutation of 0 to 127; slot s belongs to the owner s // (128 // 16) along freq.
All inputs are finite; a program needn't handle non-finite values.
Results may differ from a plain program's by a relative error of at most 0.0003.
Values may be sent and summed in bfloat16 or wider, within the bound.
A program may use at most 64 MiB of HBM per device.

v0:
```python
import functools
import math

import jax
import jax.numpy as jnp
from jax import lax
from jax.experimental import pallas as pl
from jax.experimental.pallas import tpu as pltpu
from jax.sharding import PartitionSpec as P

ORBS = 5
TILE = 128
STEP = 32

HIGH = lax.Precision.HIGHEST
BETA_INV = 0.1

OUTER = (((0,), (0,)), ((), ()))
ROWS = (((1,), (1,)), ((), ()))


def halves(value):
    top = value.astype(jnp.bfloat16)
    return top, (value - top.astype(jnp.float32)).astype(jnp.bfloat16)


def dot(a, b, dims=(((1,), (0,)), ((), ()))):
    return lax.dot_general(a, b, dims, preferred_element_type=jnp.float32)


def small_inverse(real, imag):
    size = real.shape[0]
    lanes = lax.broadcasted_iota(jnp.int32, (1, size), 1)
    rows = lax.broadcasted_iota(jnp.int32, (size, 1), 0)
    for k in range(size):
        here = lanes == k
        down = rows == k
        pr, pi = real[k : k + 1, k : k + 1], imag[k : k + 1, k : k + 1]
        scale = 1.0 / (pr * pr + pi * pi)
        qr, qi = pr * scale, -pi * scale
        cr = jnp.where(down, 1.0, real[:, k : k + 1])
        ci = jnp.where(down, 0.0, imag[:, k : k + 1])
        rr = jnp.where(here, 1.0, real[k : k + 1, :])
        ri = jnp.where(here, 0.0, imag[k : k + 1, :])
        sr = rr * qr - ri * qi
        si = rr * qi + ri * qr
        cross = here | down
        real = jnp.where(cross, 0.0, real) - (cr * sr - ci * si)
        imag = jnp.where(cross, 0.0, imag) - (cr * si + ci * sr)
    return real, imag


def sweep(mr, mi, bands):
    eye = (
        lax.broadcasted_iota(jnp.int32, (STEP, STEP), 0)
        == lax.broadcasted_iota(jnp.int32, (STEP, STEP), 1)
    ).astype(jnp.float32)
    lane = lax.broadcasted_iota(jnp.int32, (STEP, TILE), 1)
    row = lax.broadcasted_iota(jnp.int32, (STEP, TILE), 0)
    wide = lax.broadcasted_iota(jnp.int32, (1, bands), 1)

    def tile_step(tile, carry):
        base = pl.multiple_of(tile * TILE, TILE)
        for part in range(TILE // STEP):
            off = part * STEP
            start = pl.multiple_of(base + off, STEP)
            own = pl.ds(start, STEP)
            cols = pl.ds(base, TILE)
            dr = mr[own, cols][:, off : off + STEP]
            di = mi[own, cols][:, off : off + STEP]
            nr, ni = small_inverse(dr, di)
            vr, vi = -nr, -ni
            place = wide - start
            inside = (place >= 0) & (place < STEP)
            unit = (
                lax.broadcasted_iota(jnp.int32, (STEP, bands), 1)
                == lax.broadcasted_iota(jnp.int32, (STEP, bands), 0) + start
            ).astype(jnp.float32)
            rr = jnp.where(inside, unit, mr[own, :])
            ri = jnp.where(inside, 0.0, mi[own, :])
            rrh, rrl = halves(rr)
            rih, ril = halves(ri)
            stack = jnp.concatenate([rrh, rrh, rrl, rih, rih, ril], axis=0)
            vrh, vrl = halves(vr)
            vih, vil = halves(vi)
            left = jnp.concatenate(
                [
                    jnp.concatenate([vrh, vrl, vrh, -vih, -vil, -vih], axis=0),
                    jnp.concatenate([vih, vil, vih, vrh, vrl, vrh], axis=0),
                ],
                axis=1,
            )
            both = dot(left, stack, OUTER)
            qr, qi = both[:STEP], both[STEP:]
            qrh, qrl = halves(qr)
            qih, qil = halves(qi)
            to_real = jnp.concatenate([qrh, qrl, qrh, -qih, -qil, -qih], axis=0)
            to_imag = jnp.concatenate([qih, qil, qih, qrh, qrl, qrh], axis=0)
            mr[...] = jnp.where(inside, 0.0, mr[...]) - dot(stack, to_real, OUTER)
            mi[...] = jnp.where(inside, 0.0, mi[...]) - dot(stack, to_imag, OUTER)
            mr[own, :] = -qr
            mi[own, :] = -qi
        return carry

    lax.fori_loop(0, bands // TILE, tile_step, 0)


def point_kernel(scalars, proj_ref, sig_ref, slot_ref, energy_ref, out_ref, mr, mi, pm):
    atoms = slot_ref.shape[1]
    orbitals, bands = proj_ref.shape
    omega, weight = scalars[0], scalars[1]
    rows = lax.broadcasted_iota(jnp.int32, (atoms, atoms), 0)
    cols = lax.broadcasted_iota(jnp.int32, (atoms, atoms), 1)
    eye = rows == cols
    turn = (rows == slot_ref[...]).astype(jnp.float32)
    sig = lax.dot_general(sig_ref[...], turn, ROWS, precision=HIGH, preferred_element_type=jnp.float32)

    proj = proj_ref[...]
    orow = lax.broadcasted_iota(jnp.int32, (atoms, orbitals), 0)
    ocol = lax.broadcasted_iota(jnp.int32, (atoms, orbitals), 1)
    for m in range(ORBS):
        pick = (ocol == orow * ORBS + m).astype(jnp.float32).astype(jnp.bfloat16)
        pm[m * atoms : (m + 1) * atoms, :] = dot(pick, proj).astype(jnp.bfloat16)
    planes = pm[...]

    def lifted(first):
        made = []
        for m in range(ORBS):
            line = [
                jnp.where(eye, sig[first + m * ORBS + o : first + m * ORBS + o + 1, :], 0.0)
                for o in range(ORBS)
            ]
            high, low = halves(jnp.concatenate(line, axis=1))
            made.append((dot(high, planes) + dot(low, planes)).astype(jnp.bfloat16))
        made = jnp.concatenate(made, axis=0)
        return dot(
            jnp.concatenate([planes, made], axis=0), jnp.concatenate([made, planes], axis=0), OUTER
        )

    diag = lax.broadcasted_iota(jnp.int32, (bands, bands), 0) == lax.broadcasted_iota(
        jnp.int32, (bands, bands), 1
    )
    mr[...] = -jnp.where(diag, energy_ref[...], 0.0) - 0.5 * lifted(0)
    mi[...] = jnp.where(diag, omega, 0.0) - 0.5 * lifted(ORBS * ORBS)

    sweep(mr, mi, bands)

    lines = []
    for ref in (mr, mi):
        high, low = halves(ref[...])
        spread = dot(planes, high) + dot(planes, low)
        for m in range(ORBS):
            vh, vl = halves(spread[m * atoms : (m + 1) * atoms, :])
            block = dot(vh, planes, ROWS) + dot(vl, planes, ROWS)
            for o in range(ORBS):
                lines.append(
                    jnp.sum(
                        jnp.where(eye, block[:, o * atoms : (o + 1) * atoms], 0.0),
                        axis=0,
                        keepdims=True,
                    )
                )
    found = jnp.concatenate(lines, axis=0) * (-weight)
    out_ref[...] = jnp.dot(found, turn, precision=HIGH, preferred_element_type=jnp.float32)


def point_blocks(scalars, proj, sig, slots, energy, **options):
    orbitals, bands = proj.shape
    vmem = pl.BlockSpec(memory_space=pltpu.VMEM)
    return pl.pallas_call(
        point_kernel,
        out_shape=jax.ShapeDtypeStruct(sig.shape, jnp.float32),
        in_specs=[pl.BlockSpec(memory_space=pltpu.SMEM)] + [vmem] * 4,
        out_specs=vmem,
        scratch_shapes=[
            pltpu.VMEM((bands, bands), jnp.float32),
            pltpu.VMEM((bands, bands), jnp.float32),
            pltpu.VMEM((orbitals, bands), jnp.bfloat16),
        ],
        compiler_params=pltpu.CompilerParams(vmem_limit_bytes=56 * 1024 * 1024),
        name="point",
        **options,
    )(scalars, proj, sig, slots, energy)


def local(band_energy, projector, sigma, atom_of_slot, kweight):
    freq_count = lax.axis_size("freq")
    freq_index = lax.axis_index("freq")
    kpt_index = lax.axis_index("kpt")
    points = band_energy.shape[0]
    atoms = atom_of_slot.shape[0]
    per_freq = sigma.shape[4] // freq_count
    projections = lax.all_gather(projector, "freq", axis=1, tiled=True)
    sig_here = lax.all_to_all(sigma, "freq", split_axis=4, concat_axis=3, tiled=True)
    weights = kweight.astype(jnp.float32)
    total = jnp.sum(weights)
    own_weights = lax.dynamic_slice_in_dim(weights, kpt_index * points, points, 0)
    slots = atom_of_slot.reshape(1, atoms)

    columns = []
    for here in range(per_freq):
        number = freq_index * per_freq + here
        omega = (2.0 * number.astype(jnp.float32) + 1.0) * math.pi * BETA_INV
        sig = sig_here[..., here].reshape(2 * ORBS * ORBS, atoms)
        summed = 0.0
        for point in range(points):
            scalars = jnp.stack([omega, own_weights[point] / total])
            summed = summed + point_blocks(
                scalars, projections[point], sig, slots, band_energy[point : point + 1]
            )
        columns.append(summed.reshape(2, ORBS, ORBS, atoms))
    partial_blocks = jnp.stack(columns, axis=4)
    owned = lax.all_to_all(partial_blocks, "freq", split_axis=3, concat_axis=4, tiled=True)
    return lax.psum_scatter(owned, "kpt", scatter_dimension=3, tiled=True)


def solution(mesh):
    placed = (P("kpt", None), P("kpt", "freq", None), P(None, None, None, "freq", None), P(), P())
    return jax.shard_map(
        local,
        mesh=mesh,
        in_specs=placed,
        out_specs=P(None, None, None, ("freq", "kpt"), None),
        check_vma=False,
    )
```

profile of v0, /device:TPU:0, one launch (start us, length us, event | category | flops | bytes accessed | tf_op | source)
XLA Modules:
  0.0 121.0 jit_solution(16522189075816179613)
XLA Ops:
  0.0 1.3 %copy.16 = f32[2,5,5,8,16]{3,2,1,0,4:T(8,128)S(1)} copy(f32[2,5,5,8,16]{4,3,2,1,0:T(8,128)} %param.7) | data formatting | bytes 51200 | tf_op args[2]
  1.3 0.9 reshape.6
  2.2 0.0 copy-start
  2.2 7.5 %all-to-all-start = ((f32[16,1,400]{2,1,0:T(1,128)}), f32[16,1,400]{2,1,0:T(1,128)S(1)}, u32[]{:S(2)}, u32[]{:S(2)}) async-start(f32[16,1,400]{2,1,0:T(1,128)} %reshape.6), calls=%async_computation | async-start | bytes 65536 | tf_op jit(solution)/shard_map/all_to_all | solution.py:194
  9.7 0.0 copy-start.1
  9.7 0.6 copy-done.1
  10.4 0.6 convert_reduce_fusion
  11.0 0.0 copy-done
  11.0 24.5 %all_gather.3 = bf16[1,640,384]{2,1,0:T(8,128)(2,1)} all-gather(bf16[1,40,384]{2,1,0:T(8,128)(2,1)S(1)} %copy-done), channel_id=1, replica_groups=mesh['freq'=16,'kpt'=2] {'freq'}, dimensions={1}, use_global_device_ids=true | all-gather | bytes 522240 | tf_op jit(solution)/shard_map/all_gather | solution.py:193
  35.5 0.6 dynamic_slice.3
  37.4 0.6 pad_maximum_fusion.scalars
  38.0 0.0 all-to-all-done
  38.0 0.6 broadcast
  38.6 0.8 reduce
  39.3 0.2 reshape.7
  39.6 0.1 copy.17
  39.7 0.8 reshape_squeeze.3.sig_ref
  40.5 53.3 %point.1 = f32[50,128]{1,0:T(8,128)} custom-call(f32[2]{0:T(128)} %pad_maximum_fusion.scalars, bf16[640,384]{1,0:T(8,128)(2,1)} %bitcast.26, f32[50,128]{1,0:T(8,128)} %reshape_squeeze.3.sig_ref, s32[1,128]{1,0:T(1,128)} %bitcast.28, f32[1,384]{1,0:T(1,128)} %energy_ref.1), custom_call_target="tpu_custom_call" | custom-call | tf_op jit(solution)/shard_map/point/pallas_call | solution.py:170
  93.8 0.8 stack_reshape.3
  94.6 0.4 copy.18
  95.0 1.7 %reshape.8 = f32[16,1,400]{2,1,0:T(1,128)} reshape(f32[128,5,1,2,5]{4,3,2,1,0:T(2,128)S(1)} %bitcast.23) | data formatting | bytes 51200
  96.7 3.5 %all-to-all-start.1 = ((f32[16,1,400]{2,1,0:T(1,128)}), f32[16,1,400]{2,1,0:T(1,128)S(1)}, u32[]{:S(2)}, u32[]{:S(2)}) async-start(f32[16,1,400]{2,1,0:T(1,128)} %reshape.8), calls=%async_computation.1 | async-start | bytes 65536 | tf_op jit(solution)/shard_map/all_to_all | solution.py:213
  100.2 0.0 copy-start.2
  100.3 0.6 copy-done.2
  100.9 0.7 dynamic-slice
  102.3 4.6 %all-to-all-done.1 = f32[16,1,400]{2,1,0:T(1,128)S(1)} async-done(((f32[16,1,400]{2,1,0:T(1,128)}), f32[16,1,400]{2,1,0:T(1,128)S(1)}, u32[]{:S(2)}, u32[]{:S(2)}) %all-to-all-start.1) | async-done | bytes 25632 | tf_op jit(solution)/shard_map/all_to_all | solution.py:213
  106.8 0.8 reduce.1
  107.6 0.9 reshape.9
  108.5 1.2 %copy.22 = f32[2,5,5,16,8,1]{4,3,0,2,1,5:T(8,128)S(1)} copy(f32[2,5,5,16,8,1]{2,0,1,4,3,5:T(2,128)S(1)} %bitcast.24) | data formatting | bytes 51200 | tf_op jit(solution)/shard_map/all_to_all | solution.py:213
  109.7 0.2 copy.20
  109.9 10.4 %all-reduce = f32[2,5,5,8,16]{4,0,2,1,3:T(2,128)S(1)} all-reduce(f32[2,5,5,8,16]{4,0,2,1,3:T(2,128)S(1)} %copy.20), channel_id=2, replica_groups=mesh['freq'=16,'kpt'=2] {'kpt'}, use_global_device_ids=true, to_apply=%region_1.0.clone | all-reduce | flops 6400 | bytes 51200
  120.3 0.7 copy.21
  (3 shorter events, 0.1 us)
Async XLA Ops:
  2.2 8.8 %copy-start = (bf16[1,40,384]{2,1,0:T(8,128)(2,1)S(1)}, bf16[1,40,384]{2,1,0:T(8,128)(2,1)}, u32[]{:S(2)}) copy-start(bf16[1,40,384]{2,1,0:T(8,128)(2,1)} %param.6) | copy-start | bytes 92164
  2.2 35.8 %all-to-all-start = ((f32[16,1,400]{2,1,0:T(1,128)}), f32[16,1,400]{2,1,0:T(1,128)S(1)}, u32[]{:S(2)}, u32[]{:S(2)}) async-start(f32[16,1,400]{2,1,0:T(1,128)} %reshape.6), calls=%async_computation | async-start | bytes 65536 | tf_op jit(solution)/shard_map/all_to_all | solution.py:194
  9.7 0.7 copy-start.1
  96.7 10.1 %all-to-all-start.1 = ((f32[16,1,400]{2,1,0:T(1,128)}), f32[16,1,400]{2,1,0:T(1,128)S(1)}, u32[]{:S(2)}, u32[]{:S(2)}) async-start(f32[16,1,400]{2,1,0:T(1,128)} %reshape.8), calls=%async_computation.1 | async-start | bytes 65536 | tf_op jit(solution)/shard_map/all_to_all | solution.py:213
  100.2 0.7 copy-start.2
where the time goes:
time: 122 us; the launch traced here: 121 us
  Pallas kernels  53.3 us (44%)
  blocking collectives  34.9 us (29%)
  local copies, waits for them, and re-layouts  12.3 us (10%)
  starting transfers between devices  11 us (9%)
  waiting for transfers between devices  4.58 us (4%)
  other arithmetic  2.74 us (2%)
  between operations  2.13 us (2%)
    pallas_call x1, Pallas kernels, point_blocks(): pl.pallas_call(point_kernel, out_shape=jax.ShapeDtypeStruct(sig.shape, jn...  53.3 us
    all_gather x1, blocking collectives, local(): projections = lax.all_gather(projector, 'freq', axis=1, tiled=True)  24.5 us
    unnamed x1, blocking collectives  10.4 us
    all_to_all x1, starting transfers between devices, local(): lax.all_to_all(sigma, 'freq', split_axis=4, concat_axis=3, tiled=True)  7.52 us
    unnamed x13, local copies, waits for them, and re-layouts  6.92 us
    all_to_all x1, waiting for transfers between devices, local(): lax.all_to_all(partial_blocks, 'freq', split_axis=3, concat_axis=4, tiled...  4.57 us
    all_to_all x1, starting transfers between devices, local(): lax.all_to_all(partial_blocks, 'freq', split_axis=3, concat_axis=4, tiled...  3.5 us
  transfers between devices with their start and end apart: 2, of which 1 were waited for; matrix products, arithmetic and copies ran while one was open for 2% of the time, Pallas kernels for 0%

commit v1 on v0

--- a/solution.py
+++ b/solution.py
@@ -10,6 +10,7 @@
 
 ORBS = 5
 TILE = 128
+MESH = pl.DeviceIdType.MESH
 STEP = 32
 
 HIGH = lax.Precision.HIGHEST
@@ -105,21 +106,26 @@
     lax.fori_loop(0, bands // TILE, tile_step, 0)
 
 
-def point_kernel(scalars, proj_ref, sig_ref, slot_ref, energy_ref, out_ref, mr, mi, pm):
+def point_kernel(point, points, kweight, proj_ref, sig_ref, slot_ref, back_ref, energy_ref, out_ref, mr, mi, pm):
     atoms = slot_ref.shape[1]
-    orbitals, bands = proj_ref.shape
-    omega, weight = scalars[0], scalars[1]
+    owners, padded, bands = proj_ref.shape
+    each = atoms // owners
+    omega = (2 * lax.axis_index("freq") + 1).astype(jnp.float32) * (math.pi * BETA_INV)
+    count = kweight.shape[0]
+    total = sum(kweight[i] for i in range(count)).astype(jnp.float32)
+    weight = kweight[lax.axis_index("kpt") * points + point].astype(jnp.float32)
     rows = lax.broadcasted_iota(jnp.int32, (atoms, atoms), 0)
     cols = lax.broadcasted_iota(jnp.int32, (atoms, atoms), 1)
     eye = rows == cols
     turn = (rows == slot_ref[...]).astype(jnp.float32)
-    sig = lax.dot_general(sig_ref[...], turn, ROWS, precision=HIGH, preferred_element_type=jnp.float32)
-
-    proj = proj_ref[...]
-    orow = lax.broadcasted_iota(jnp.int32, (atoms, orbitals), 0)
-    ocol = lax.broadcasted_iota(jnp.int32, (atoms, orbitals), 1)
+    sig = jnp.dot(turn, sig_ref[...], precision=HIGH, preferred_element_type=jnp.float32).T
+
+    proj = proj_ref[...].reshape(owners * padded, bands)
+    orow = lax.broadcasted_iota(jnp.int32, (atoms, owners * padded), 0)
+    ocol = lax.broadcasted_iota(jnp.int32, (atoms, owners * padded), 1)
+    target = ocol - (lax.div(orow, each) * padded + lax.rem(orow, each) * ORBS)
     for m in range(ORBS):
-        pick = (ocol == orow * ORBS + m).astype(jnp.float32).astype(jnp.bfloat16)
+        pick = (target == m).astype(jnp.float32).astype(jnp.bfloat16)
         pm[m * atoms : (m + 1) * atoms, :] = dot(pick, proj).astype(jnp.bfloat16)
     planes = pm[...]
 
@@ -160,58 +166,251 @@
                         keepdims=True,
                     )
                 )
-    found = jnp.concatenate(lines, axis=0) * (-weight)
-    out_ref[...] = jnp.dot(found, turn, precision=HIGH, preferred_element_type=jnp.float32)
-
-
-def point_blocks(scalars, proj, sig, slots, energy, **options):
-    orbitals, bands = proj.shape
+    scale = jnp.full((1, 1), weight) / jnp.full((1, 1), total)
+    found = jnp.concatenate(lines, axis=0) * -scale
+    back = (rows == back_ref[...]).astype(jnp.float32)
+    out_ref[...] = jnp.dot(found, back, precision=HIGH, preferred_element_type=jnp.float32).T
+
+
+def point_blocks(point, points, kweight, proj, sig, slots, back, energy):
+    owners, padded, bands = proj.shape
+    atoms = slots.shape[1]
     vmem = pl.BlockSpec(memory_space=pltpu.VMEM)
     return pl.pallas_call(
-        point_kernel,
+        functools.partial(point_kernel, point, points),
         out_shape=jax.ShapeDtypeStruct(sig.shape, jnp.float32),
-        in_specs=[pl.BlockSpec(memory_space=pltpu.SMEM)] + [vmem] * 4,
+        in_specs=[pl.BlockSpec(memory_space=pltpu.SMEM)] + [vmem] * 5,
         out_specs=vmem,
         scratch_shapes=[
             pltpu.VMEM((bands, bands), jnp.float32),
             pltpu.VMEM((bands, bands), jnp.float32),
-            pltpu.VMEM((orbitals, bands), jnp.bfloat16),
+            pltpu.VMEM((ORBS * atoms, bands), jnp.bfloat16),
         ],
         compiler_params=pltpu.CompilerParams(vmem_limit_bytes=56 * 1024 * 1024),
         name="point",
-        **options,
-    )(scalars, proj, sig, slots, energy)
+    )(kweight, proj, sig, slots, back, energy)
+
+
+def radices(count):
+    made = []
+    for radix in (2, 2):
+        if count % radix == 0:
+            made.insert(0, radix)
+            count //= radix
+    while count > 1:
+        radix = 4 if count % 4 == 0 else count
+        made.insert(0, radix)
+        count //= radix
+    return made
+
+
+def greet(axis):
+    count, me = lax.axis_size(axis), lax.axis_index(axis)
+    barrier = pltpu.get_barrier_semaphore()
+    for j in range(1, count):
+        pl.semaphore_signal(
+            barrier, inc=1, device_id={axis: lax.rem(me + j, count)}, device_id_type=MESH
+        )
+    return barrier, count - 1
+
+
+def gather_kernel(proj_ref, sig_ref, proj_out, sig_out, proj_send, proj_recv, sig_send, sig_recv):
+    count, me = lax.axis_size("freq"), lax.axis_index("freq")
+    barrier, peers = greet("freq")
+    points, rows, bands = proj_ref.shape
+    padded = proj_out.shape[2]
+    own = proj_ref[...]
+    if padded > rows:
+        own = jnp.concatenate([own, jnp.zeros((points, padded - rows, bands), own.dtype)], axis=1)
+    proj_out[me] = own
+    sig_out[me] = sig_ref[me]
+    pl.semaphore_wait(barrier, peers)
+
+    dims = radices(count)
+    strides = [math.prod(dims[s + 1 :]) for s in range(len(dims))]
+
+    def shifted(index, s, j):
+        digit = lax.rem(lax.div(index, strides[s]), dims[s])
+        return index + (lax.rem(digit + j, dims[s]) - digit) * strides[s]
+
+    def block(owner, target, slot):
+        return pltpu.make_async_remote_copy(
+            src_ref=proj_out.at[owner],
+            dst_ref=proj_out.at[owner],
+            send_sem=proj_send.at[slot],
+            recv_sem=proj_recv.at[owner],
+            device_id={"freq": target},
+            device_id_type=MESH,
+        )
+
+    sent = []
+
+    def forward(owner, first):
+        for s in range(first, len(dims)):
+            for j in range(1, dims[s]):
+                copy = block(owner, shifted(me, s, j), len(sent))
+                copy.start()
+                sent.append(copy)
+
+    forward(me, 0)
+    parts = []
+    for j in range(1, count):
+        target = lax.rem(me + j, count)
+        copy = pltpu.make_async_remote_copy(
+            src_ref=sig_ref.at[target],
+            dst_ref=sig_out.at[me],
+            send_sem=sig_send.at[j],
+            recv_sem=sig_recv.at[me],
+            device_id={"freq": target},
+            device_id_type=MESH,
+        )
+        copy.start()
+        parts.append(copy)
+    got = [me]
+    for s in range(len(dims)):
+        fresh = []
+        for j in range(1, dims[s]):
+            for base in got:
+                owner = shifted(base, s, j)
+                block(owner, owner, 0).wait_recv()
+                forward(owner, s + 1)
+                fresh.append(owner)
+        got += fresh
+    for j in range(1, count):
+        source = lax.rem(me + j, count)
+        pltpu.make_async_remote_copy(
+            src_ref=sig_ref.at[source],
+            dst_ref=sig_out.at[source],
+            send_sem=sig_send.at[j],
+            recv_sem=sig_recv.at[source],
+            device_id={"freq": source},
+            device_id_type=MESH,
+        ).wait_recv()
+    for copy in sent + parts:
+        copy.wait_send()
+
+
+def gather(proj, sig, count):
+    points, rows, bands = proj.shape
+    padded = -(-rows // 16) * 16
+    vmem = pl.BlockSpec(memory_space=pltpu.VMEM)
+    return pl.pallas_call(
+        gather_kernel,
+        out_shape=(
+            jax.ShapeDtypeStruct((count, points, padded, bands), proj.dtype),
+            jax.ShapeDtypeStruct(sig.shape, sig.dtype),
+        ),
+        in_specs=[vmem, vmem],
+        out_specs=(vmem, vmem),
+        scratch_shapes=[pltpu.SemaphoreType.DMA((count,))] * 4,
+        compiler_params=pltpu.CompilerParams(
+            collective_id=0, has_side_effects=True, vmem_limit_bytes=32 * 1024 * 1024
+        ),
+        name="gather",
+    )(proj, sig)
+
+
+def exchange_kernel(mine_ref, out_ref, theirs, summed, kpt_sems, freq_send, freq_recv):
+    count, me = lax.axis_size("freq"), lax.axis_index("freq")
+    others, point = lax.axis_size("kpt"), lax.axis_index("kpt")
+    _, peers = greet("freq")
+    barrier, more = greet("kpt")
+    pl.semaphore_wait(barrier, peers + more)
+    kpt_send, kpt_recv = kpt_sems.at[0], kpt_sems.at[1]
+    copies = []
+    for j in range(1, others):
+        target = lax.rem(point + j, others)
+        copy = pltpu.make_async_remote_copy(
+            src_ref=mine_ref.at[target],
+            dst_ref=theirs.at[j],
+            send_sem=kpt_send.at[j],
+            recv_sem=kpt_recv.at[j],
+            device_id={"kpt": target},
+            device_id_type=MESH,
+        )
+        copy.start()
+        copies.append(copy)
+    total = mine_ref[point]
+    for j in range(1, others):
+        copies[j - 1].wait()
+        total = total + theirs[j]
+    each = summed.shape[1]
+    for owner in range(count):
+        summed[owner] = total[owner * each : (owner + 1) * each]
+    copies = []
+    for j in range(1, count):
+        target = lax.rem(me + j, count)
+        copy = pltpu.make_async_remote_copy(
+            src_ref=summed.at[target],
+            dst_ref=out_ref.at[me],
+            send_sem=freq_send.at[j],
+            recv_sem=freq_recv.at[me],
+            device_id={"freq": target},
+            device_id_type=MESH,
+        )
+        copy.start()
+        copies.append(copy)
+    out_ref[me] = summed[me]
+    for j in range(1, count):
+        source = lax.rem(me + j, count)
+        pltpu.make_async_remote_copy(
+            src_ref=summed.at[source],
+            dst_ref=out_ref.at[source],
+            send_sem=freq_send.at[j],
+            recv_sem=freq_recv.at[source],
+            device_id={"freq": source},
+            device_id_type=MESH,
+        ).wait_recv()
+    for copy in copies:
+        copy.wait_send()
+
+
+def exchange(blocks, count, others):
+    atoms, kinds = blocks.shape
+    each = atoms // (count * others)
+    vmem = pl.BlockSpec(memory_space=pltpu.VMEM)
+    return pl.pallas_call(
+        exchange_kernel,
+        out_shape=jax.ShapeDtypeStruct((count, each, kinds), blocks.dtype),
+        in_specs=[vmem],
+        out_specs=vmem,
+        scratch_shapes=[
+            pltpu.VMEM((others, atoms // others, kinds), blocks.dtype),
+            pltpu.VMEM((count, each, kinds), blocks.dtype),
+            pltpu.SemaphoreType.DMA((2, others)),
+            pltpu.SemaphoreType.DMA((count,)),
+            pltpu.SemaphoreType.DMA((count,)),
+        ],
+        compiler_params=pltpu.CompilerParams(collective_id=1, has_side_effects=True),
+        name="exchange",
+    )(blocks.reshape(others, atoms // others, kinds))
 
 
 def local(band_energy, projector, sigma, atom_of_slot, kweight):
-    freq_count = lax.axis_size("freq")
-    freq_index = lax.axis_index("freq")
-    kpt_index = lax.axis_index("kpt")
+    count, others = lax.axis_size("freq"), lax.axis_size("kpt")
     points = band_energy.shape[0]
     atoms = atom_of_slot.shape[0]
-    per_freq = sigma.shape[4] // freq_count
-    projections = lax.all_gather(projector, "freq", axis=1, tiled=True)
-    sig_here = lax.all_to_all(sigma, "freq", split_axis=4, concat_axis=3, tiled=True)
-    weights = kweight.astype(jnp.float32)
-    total = jnp.sum(weights)
-    own_weights = lax.dynamic_slice_in_dim(weights, kpt_index * points, points, 0)
-    slots = atom_of_slot.reshape(1, atoms)
-
-    columns = []
-    for here in range(per_freq):
-        number = freq_index * per_freq + here
-        omega = (2.0 * number.astype(jnp.float32) + 1.0) * math.pi * BETA_INV
-        sig = sig_here[..., here].reshape(2 * ORBS * ORBS, atoms)
-        summed = 0.0
-        for point in range(points):
-            scalars = jnp.stack([omega, own_weights[point] / total])
-            summed = summed + point_blocks(
-                scalars, projections[point], sig, slots, band_energy[point : point + 1]
-            )
-        columns.append(summed.reshape(2, ORBS, ORBS, atoms))
-    partial_blocks = jnp.stack(columns, axis=4)
-    owned = lax.all_to_all(partial_blocks, "freq", split_axis=3, concat_axis=4, tiled=True)
-    return lax.psum_scatter(owned, "kpt", scatter_dimension=3, tiled=True)
+    kinds = 2 * ORBS * ORBS
+    slots = sigma.shape[3]
+    sig = jnp.transpose(sigma.reshape(kinds, slots, count), (2, 1, 0))
+    projections, sig = gather(projector, sig, count)
+    sig = sig.reshape(atoms, kinds)
+    order = atom_of_slot.reshape(count, others, -1).transpose(1, 0, 2).reshape(1, atoms)
+    summed = None
+    for point in range(points):
+        block = point_blocks(
+            point,
+            points,
+            kweight,
+            projections[:, point],
+            sig,
+            atom_of_slot.reshape(1, atoms),
+            order,
+            band_energy[point : point + 1],
+        )
+        summed = block if summed is None else summed + block
+    owned = exchange(summed, count, others)
+    return jnp.transpose(owned, (2, 1, 0)).reshape(2, ORBS, ORBS, -1, count)
 
 
 def solution(mesh):

time: 122 us -> 86.6 us (0.71)
  blocking collectives: 34.9 us -> 0 us
  Pallas kernels: 53.3 us -> 80.9 us
  starting transfers between devices: 11 us -> 0 us
  local copies, waits for them, and re-layouts: 12.3 us -> 5.42 us
  waiting for transfers between devices: 4.58 us -> 0 us
  other arithmetic: 2.74 us -> 0 us
  between operations: 2.13 us -> 0.06 us
    pallas_call x1 -> x3, Pallas kernels: 53.3 us -> 80.9 us  [the longest x1 53.5 us: point_blocks(): pl.pallas_call(functools.partial(point_kernel, point, points), out_shape=...]
    all_gather x1 -> x0, blocking collectives: 24.5 us -> none  [local(): projections = lax.all_gather(projector, 'freq', axis=1, tiled=True)]
    all_to_all x2 -> x0, starting transfers between devices: 11 us -> none  [the longest x1 7.52 us: local(): lax.all_to_all(sigma, 'freq', split_axis=4, concat_axis=3, tiled=True)]
    unnamed x1 -> x0, blocking collectives: 10.4 us -> none
    unnamed x13 -> x8, local copies, waits for them, and re-layouts: 6.92 us -> 2.11 us
    all_to_all x2 -> x0, waiting for transfers between devices: 4.58 us -> none  [the longest x1 4.57 us: local(): lax.all_to_all(partial_blocks, 'freq', split_axis=3, concat_axis=4, tiled...]
    all_to_all x5 -> x0, local copies, waits for them, and re-layouts: 2.19 us -> none  [the longest x2 1.43 us: local(): lax.all_to_all(partial_blocks, 'freq', split_axis=3, concat_axis=4, tiled...]
    another operation x3 -> x0, local copies, waits for them, and re-layouts: 1.96 us -> none  [the longest x2 1.15 us: local(): partial_blocks = jnp.stack(columns, axis=4)]
  transfers between devices with their start and end apart: 2 -> 0, of which waited for: 1 -> 0; matrix products, arithmetic and copies ran while one was open for 2% -> 0% of each run, Pallas kernels for 0% -> 0%
where the time goes in v1:
time: 86.6 us; the launch traced here: 86.4 us
  Pallas kernels  80.9 us (93%)
  local copies, waits for them, and re-layouts  5.42 us (6%)
    pallas_call x1, Pallas kernels, point_blocks(): pl.pallas_call(functools.partial(point_kernel, point, points), out_shape=...  53.5 us
    pallas_call x1, Pallas kernels, gather(): pl.pallas_call(gather_kernel, out_shape=(jax.ShapeDtypeStruct((count, poi...  15.2 us
    pallas_call x1, Pallas kernels, exchange(): pl.pallas_call(exchange_kernel, out_shape=jax.ShapeDtypeStruct((count, ea...  12.2 us
    unnamed x8, local copies, waits for them, and re-layouts  2.11 us

profile of v1, /device:TPU:0, one launch (start us, length us, event | category | flops | bytes accessed | tf_op | source)
XLA Modules:
  0.0 86.4 jit_solution(17776603996134485806)
XLA Ops:
  0.0 0.0 copy-start.2
  0.0 1.1 %copy.9 = f32[50,8,16]{0,1,2:T(8,128)S(1)} copy(f32[50,8,16]{2,1,0:T(8,128)} %bitcast.13) | data formatting | bytes 51200 | tf_op jit(solution)/shard_map/reshape | solution.py:395
  1.1 0.0 copy-done.2
  1.1 15.2 %gather.1 = (bf16[16,1,48,384]{3,2,1,0:T(8,128)(2,1)S(1)}, f32[16,8,50]{2,1,0:T(8,128)S(1)}) custom-call(bf16[1,40,384]{2,1,0:T(8,128)(2,1)S(1)} %copy-done.2, f32[16,8,50]{2,1,0:T(8,128)S(1)} %bitcast.10), custom_call_target="tpu_custom_call" | custom-call | tf_op jit(solution)/shard_map/gather/pallas_call | solution.py:297
  16.3 0.0 copy-start
  16.3 0.8 copy-done
  17.1 0.0 copy-start.1
  17.1 0.6 copy-done.1
  17.7 0.0 copy-start.3
  17.7 0.7 copy-done.3
  18.4 0.1 reshape.24
  18.5 0.6 reshape.25.back_ref
  19.1 53.5 %point.1 = f32[128,50]{1,0:T(8,128)} custom-call(s32[2]{0:T(128)} %kweight.1, bf16[16,48,384]{2,1,0:T(8,128)(2,1)} %bitcast.9, f32[128,50]{1,0:T(8,128)} %bitcast.11, s32[1,128]{1,0:T(1,128)} %bitcast.16, s32[1,128]{1,0:T(1,128)} %reshape.25.back_ref, f32[1,384]{1,0:T(1,128)} %energy_ref.1), custom_call_target="tpu_custom_call" | custom-call | tf_op jit(solution)/shard_map/point/pallas_call | solution.py:179
  72.7 12.2 %exchange.1 = f32[16,4,50]{2,1,0:T(4,128)} custom-call(f32[2,64,50]{2,1,0:T(8,128)} %bitcast.12), custom_call_target="tpu_custom_call" | custom-call | tf_op jit(solution)/shard_map/exchange/pallas_call | solution.py:372
  84.9 1.5 %copy.11 = f32[50,4,16]{2,1,0:T(4,128)} copy(f32[50,4,16]{0,1,2:T(4,128)} %bitcast.14) | data formatting | bytes 25600 | tf_op jit(solution)/shard_map/transpose | solution.py:413
  (1 shorter events, 0.0 us)
Async XLA Ops:
  0.0 1.1 %copy-start.2 = (bf16[1,40,384]{2,1,0:T(8,128)(2,1)S(1)}, bf16[1,40,384]{2,1,0:T(8,128)(2,1)}, u32[]{:S(2)}) copy-start(bf16[1,40,384]{2,1,0:T(8,128)(2,1)} %proj_ref.1) | copy-start | bytes 92164
  16.3 0.8 copy-start
  17.1 0.6 copy-start.1
  17.7 0.7 copy-start.3

commit v2 on v1

--- a/solution.py
+++ b/solution.py
@@ -29,26 +29,108 @@
     return lax.dot_general(a, b, dims, preferred_element_type=jnp.float32)
 
 
+def times(a, b):
+    return a[0] * b[0] - a[1] * b[1], a[0] * b[1] + a[1] * b[0]
+
+
+def plus(a, b):
+    return a[0] + b[0], a[1] + b[1]
+
+
+def minus(a, b):
+    return a[0] - b[0], a[1] - b[1]
+
+
+def pair_inverse(a, b, d):
+    det = minus(times(a, d), times(b, b))
+    scale = 1.0 / (det[0] * det[0] + det[1] * det[1])
+    turned = (det[0] * scale, -det[1] * scale)
+    low = times(b, turned)
+    return times(d, turned), (-low[0], -low[1]), times(a, turned)
+
+
+def quad_inverse(e):
+    a, b, d = pair_inverse(e[0][0], e[1][0], e[1][1])
+    t = [[plus(times(x, e[j][0]), times(y, e[j][1])) for j in (2, 3)] for x, y in ((a, b), (b, d))]
+    rest = {}
+    for i in (2, 3):
+        for j in (2, 3):
+            if j <= i:
+                taken = plus(times(e[i][0], t[0][j - 2]), times(e[i][1], t[1][j - 2]))
+                rest[i, j] = minus(e[i][j], taken)
+    f, g, h = pair_inverse(rest[2, 2], rest[3, 2], rest[3, 3])
+    n = [[plus(times(p[0], x), times(p[1], y)) for x, y in ((f, g), (g, h))] for p in t]
+    top = [
+        plus(a, plus(times(n[0][0], t[0][0]), times(n[0][1], t[0][1]))),
+        plus(b, plus(times(n[0][0], t[1][0]), times(n[0][1], t[1][1]))),
+        plus(d, plus(times(n[1][0], t[1][0]), times(n[1][1], t[1][1]))),
+    ]
+    neg = [[(-x[0], -x[1]) for x in line] for line in n]
+    return [
+        [top[0], top[1], neg[0][0], neg[0][1]],
+        [top[1], top[2], neg[1][0], neg[1][1]],
+        [neg[0][0], neg[1][0], f, g],
+        [neg[0][1], neg[1][1], g, h],
+    ]
+
+
 def small_inverse(real, imag):
     size = real.shape[0]
-    lanes = lax.broadcasted_iota(jnp.int32, (1, size), 1)
-    rows = lax.broadcasted_iota(jnp.int32, (size, 1), 0)
-    for k in range(size):
-        here = lanes == k
-        down = rows == k
-        pr, pi = real[k : k + 1, k : k + 1], imag[k : k + 1, k : k + 1]
-        scale = 1.0 / (pr * pr + pi * pi)
-        qr, qi = pr * scale, -pi * scale
-        cr = jnp.where(down, 1.0, real[:, k : k + 1])
-        ci = jnp.where(down, 0.0, imag[:, k : k + 1])
-        rr = jnp.where(here, 1.0, real[k : k + 1, :])
-        ri = jnp.where(here, 0.0, imag[k : k + 1, :])
-        sr = rr * qr - ri * qi
-        si = rr * qi + ri * qr
-        cross = here | down
-        real = jnp.where(cross, 0.0, real) - (cr * sr - ci * si)
-        imag = jnp.where(cross, 0.0, imag) - (cr * si + ci * sr)
-    return real, imag
+    shape = (8, size)
+    lanes = lax.broadcasted_iota(jnp.int32, shape, 1)
+    rows = lax.broadcasted_iota(jnp.int32, shape, 0)
+    parts = [
+        [(m[h : h + 8, :]) for m in (real, imag)] for h in range(0, size, 8)
+    ]
+    for k in range(0, size, 4):
+        own, off = k // 8, k % 8
+        here = (lanes >= k) & (lanes < k + 4)
+        down = (rows >= off) & (rows < off + 4)
+        cols = [
+            [
+                tuple(jnp.broadcast_to(m[:, k + j : k + j + 1], shape) for m in part)
+                for part in parts
+            ]
+            for j in range(4)
+        ]
+        e = [
+            [
+                tuple(jnp.broadcast_to(m[off + i : off + i + 1, :], shape) for m in cols[j][own])
+                for j in range(i + 1)
+            ]
+            for i in range(4)
+        ]
+        line = []
+        for i in range(4):
+            r, v = (jnp.broadcast_to(m[off + i : off + i + 1, :], shape) for m in parts[own])
+            line.append(
+                (
+                    jnp.where(here, (lanes == k + i).astype(jnp.float32), r),
+                    jnp.where(here, 0.0, v),
+                )
+            )
+        inverse = quad_inverse(e)
+        solved = []
+        for i in range(4):
+            value = times(inverse[i][0], line[0])
+            for j in range(1, 4):
+                value = plus(value, times(inverse[i][j], line[j]))
+            solved.append(value)
+        fresh = []
+        for h, part in enumerate(parts):
+            gone = here | down if h == own else here
+            value = tuple(jnp.where(gone, 0.0, m) for m in part)
+            for j in range(4):
+                col = cols[j][h]
+                if h == own:
+                    col = (
+                        jnp.where(down, (rows == off + j).astype(jnp.float32), col[0]),
+                        jnp.where(down, 0.0, col[1]),
+                    )
+                value = minus(value, times(col, solved[j]))
+            fresh.append(value)
+        parts = fresh
+    return tuple(jnp.concatenate([p[x] for p in parts], axis=0) for x in range(2))
 
 
 def sweep(mr, mi, bands):
@@ -151,21 +233,20 @@
 
     sweep(mr, mi, bands)
 
-    lines = []
-    for ref in (mr, mi):
+    lines = {}
+    for which, ref in enumerate((mr, mi)):
         high, low = halves(ref[...])
         spread = dot(planes, high) + dot(planes, low)
         for m in range(ORBS):
             vh, vl = halves(spread[m * atoms : (m + 1) * atoms, :])
-            block = dot(vh, planes, ROWS) + dot(vl, planes, ROWS)
-            for o in range(ORBS):
-                lines.append(
-                    jnp.sum(
-                        jnp.where(eye, block[:, o * atoms : (o + 1) * atoms], 0.0),
-                        axis=0,
-                        keepdims=True,
-                    )
+            rest = planes[m * atoms :, :]
+            block = dot(vh, rest, ROWS) + dot(vl, rest, ROWS)
+            for o in range(m, ORBS):
+                part = block[:, (o - m) * atoms : (o - m + 1) * atoms]
+                lines[which, m, o] = lines[which, o, m] = jnp.sum(
+                    jnp.where(eye, part, 0.0), axis=0, keepdims=True
                 )
+    lines = [lines[w, m, o] for w in range(2) for m in range(ORBS) for o in range(ORBS)]
     scale = jnp.full((1, 1), weight) / jnp.full((1, 1), total)
     found = jnp.concatenate(lines, axis=0) * -scale
     back = (rows == back_ref[...]).astype(jnp.float32)

time: 86.6 us -> 71.1 us (0.82)
  Pallas kernels: 80.9 us -> 65.4 us
    pallas_call x1, Pallas kernels: 53.5 us -> 38 us  [point_blocks(): pl.pallas_call(functools.partial(point_kernel, point, points), out_shape=...]
where the time goes in v2:
time: 71.1 us; the launch traced here: 70.9 us
  Pallas kernels  65.4 us (92%)
  local copies, waits for them, and re-layouts  5.42 us (8%)
    pallas_call x1, Pallas kernels, point_blocks(): pl.pallas_call(functools.partial(point_kernel, point, points), out_shape=...  38 us
    pallas_call x1, Pallas kernels, gather(): pl.pallas_call(gather_kernel, out_shape=(jax.ShapeDtypeStruct((count, poi...  15.2 us
    pallas_call x1, Pallas kernels, exchange(): pl.pallas_call(exchange_kernel, out_shape=jax.ShapeDtypeStruct((count, ea...  12.2 us
    unnamed x8, local copies, waits for them, and re-layouts  2.11 us
    transpose x1, local copies, waits for them, and re-layouts, local(): return jnp.transpose(owned, (2, 1, 0)).reshape(2, ORBS, ORBS, -1, count)  1.51 us

profile of v2, /device:TPU:0, one launch (start us, length us, event | category | flops | bytes accessed | tf_op | source)
XLA Modules:
  0.0 70.9 jit_solution(13739322014894432683)
XLA Ops:
  0.0 0.0 copy-start.2
  0.0 1.1 %copy.9 = f32[50,8,16]{0,1,2:T(8,128)S(1)} copy(f32[50,8,16]{2,1,0:T(8,128)} %bitcast.13) | data formatting | bytes 51200 | tf_op jit(solution)/shard_map/reshape | solution.py:476
  1.1 0.0 copy-done.2
  1.1 15.2 %gather.1 = (bf16[16,1,48,384]{3,2,1,0:T(8,128)(2,1)S(1)}, f32[16,8,50]{2,1,0:T(8,128)S(1)}) custom-call(bf16[1,40,384]{2,1,0:T(8,128)(2,1)S(1)} %copy-done.2, f32[16,8,50]{2,1,0:T(8,128)S(1)} %bitcast.10), custom_call_target="tpu_custom_call" | custom-call | tf_op jit(solution)/shard_map/gather/pallas_call | solution.py:378
  16.3 0.0 copy-start
  16.3 0.8 %copy-done = bf16[16,1,48,384]{3,2,1,0:T(8,128)(2,1)} copy-done((bf16[16,1,48,384]{3,2,1,0:T(8,128)(2,1)}, bf16[16,1,48,384]{3,2,1,0:T(8,128)(2,1)S(1)}, u32[]{:S(2)}) %copy-start) | copy-done | bytes 589848
  17.1 0.0 copy-start.1
  17.1 0.6 copy-done.1
  17.7 0.0 copy-start.3
  17.7 0.7 copy-done.3
  18.4 0.1 reshape.24
  18.5 0.6 reshape.25.back_ref
  19.1 38.0 %point.1 = f32[128,50]{1,0:T(8,128)} custom-call(s32[2]{0:T(128)} %kweight.1, bf16[16,48,384]{2,1,0:T(8,128)(2,1)} %bitcast.9, f32[128,50]{1,0:T(8,128)} %bitcast.11, s32[1,128]{1,0:T(1,128)} %bitcast.16, s32[1,128]{1,0:T(1,128)} %reshape.25.back_ref, f32[1,384]{1,0:T(1,128)} %energy_ref.1), custom_call_target="tpu_custom_call" | custom-call | tf_op jit(solution)/shard_map/point/pallas_call | solution.py:260
  57.1 12.2 %exchange.1 = f32[16,4,50]{2,1,0:T(4,128)} custom-call(f32[2,64,50]{2,1,0:T(8,128)} %bitcast.12), custom_call_target="tpu_custom_call" | custom-call | tf_op jit(solution)/shard_map/exchange/pallas_call | solution.py:453
  69.4 1.5 %copy.11 = f32[50,4,16]{2,1,0:T(4,128)} copy(f32[50,4,16]{0,1,2:T(4,128)} %bitcast.14) | data formatting | bytes 25600 | tf_op jit(solution)/shard_map/transpose | solution.py:494
  (1 shorter events, 0.0 us)
Async XLA Ops:
  0.0 1.1 %copy-start.2 = (bf16[1,40,384]{2,1,0:T(8,128)(2,1)S(1)}, bf16[1,40,384]{2,1,0:T(8,128)(2,1)}, u32[]{:S(2)}) copy-start(bf16[1,40,384]{2,1,0:T(8,128)(2,1)} %proj_ref.1) | copy-start | bytes 92164
  16.3 0.8 %copy-start = (bf16[16,1,48,384]{3,2,1,0:T(8,128)(2,1)}, bf16[16,1,48,384]{3,2,1,0:T(8,128)(2,1)S(1)}, u32[]{:S(2)}) copy-start(bf16[16,1,48,384]{3,2,1,0:T(8,128)(2,1)S(1)} %get-tuple-element.7) | copy-start | bytes 1769476
  17.1 0.6 copy-start.1
  17.7 0.7 copy-start.3

commit v3 on v2

--- a/solution.py
+++ b/solution.py
@@ -188,9 +188,9 @@
     lax.fori_loop(0, bands // TILE, tile_step, 0)
 
 
-def point_kernel(point, points, kweight, proj_ref, sig_ref, slot_ref, back_ref, energy_ref, out_ref, mr, mi, pm):
-    atoms = slot_ref.shape[1]
-    owners, padded, bands = proj_ref.shape
+def point_blocks(point, points, kweight, proj, sig_all, slot_ref, back_ref, energy_ref, mr, mi, pm):
+    atoms = back_ref.shape[1]
+    owners, padded, bands = proj.shape
     each = atoms // owners
     omega = (2 * lax.axis_index("freq") + 1).astype(jnp.float32) * (math.pi * BETA_INV)
     count = kweight.shape[0]
@@ -199,10 +199,12 @@
     rows = lax.broadcasted_iota(jnp.int32, (atoms, atoms), 0)
     cols = lax.broadcasted_iota(jnp.int32, (atoms, atoms), 1)
     eye = rows == cols
-    turn = (rows == slot_ref[...]).astype(jnp.float32)
-    sig = jnp.dot(turn, sig_ref[...], precision=HIGH, preferred_element_type=jnp.float32).T
-
-    proj = proj_ref[...].reshape(owners * padded, bands)
+    held = slot_ref.shape[1]
+    turn = (lax.broadcasted_iota(jnp.int32, (atoms, held), 0) == slot_ref[...]).astype(jnp.float32)
+    sig = sig_all[...].reshape(held, sig_all.shape[2])
+    sig = jnp.dot(turn, sig, precision=HIGH, preferred_element_type=jnp.float32).T
+
+    proj = proj.reshape(owners * padded, bands)
     orow = lax.broadcasted_iota(jnp.int32, (atoms, owners * padded), 0)
     ocol = lax.broadcasted_iota(jnp.int32, (atoms, owners * padded), 1)
     target = ocol - (lax.div(orow, each) * padded + lax.rem(orow, each) * ORBS)
@@ -228,7 +230,7 @@
     diag = lax.broadcasted_iota(jnp.int32, (bands, bands), 0) == lax.broadcasted_iota(
         jnp.int32, (bands, bands), 1
     )
-    mr[...] = -jnp.where(diag, energy_ref[...], 0.0) - 0.5 * lifted(0)
+    mr[...] = -jnp.where(diag, energy_ref[point : point + 1, :], 0.0) - 0.5 * lifted(0)
     mi[...] = jnp.where(diag, omega, 0.0) - 0.5 * lifted(ORBS * ORBS)
 
     sweep(mr, mi, bands)
@@ -250,26 +252,7 @@
     scale = jnp.full((1, 1), weight) / jnp.full((1, 1), total)
     found = jnp.concatenate(lines, axis=0) * -scale
     back = (rows == back_ref[...]).astype(jnp.float32)
-    out_ref[...] = jnp.dot(found, back, precision=HIGH, preferred_element_type=jnp.float32).T
-
-
-def point_blocks(point, points, kweight, proj, sig, slots, back, energy):
-    owners, padded, bands = proj.shape
-    atoms = slots.shape[1]
-    vmem = pl.BlockSpec(memory_space=pltpu.VMEM)
-    return pl.pallas_call(
-        functools.partial(point_kernel, point, points),
-        out_shape=jax.ShapeDtypeStruct(sig.shape, jnp.float32),
-        in_specs=[pl.BlockSpec(memory_space=pltpu.SMEM)] + [vmem] * 5,
-        out_specs=vmem,
-        scratch_shapes=[
-            pltpu.VMEM((bands, bands), jnp.float32),
-            pltpu.VMEM((bands, bands), jnp.float32),
-            pltpu.VMEM((ORBS * atoms, bands), jnp.bfloat16),
-        ],
-        compiler_params=pltpu.CompilerParams(vmem_limit_bytes=56 * 1024 * 1024),
-        name="point",
-    )(kweight, proj, sig, slots, back, energy)
+    return jnp.dot(found, back, precision=HIGH, preferred_element_type=jnp.float32).T
 
 
 def radices(count):
@@ -285,19 +268,19 @@
     return made
 
 
-def greet(axis):
+def greet(barrier, axis):
     count, me = lax.axis_size(axis), lax.axis_index(axis)
-    barrier = pltpu.get_barrier_semaphore()
     for j in range(1, count):
         pl.semaphore_signal(
             barrier, inc=1, device_id={axis: lax.rem(me + j, count)}, device_id_type=MESH
         )
-    return barrier, count - 1
-
-
-def gather_kernel(proj_ref, sig_ref, proj_out, sig_out, proj_send, proj_recv, sig_send, sig_recv):
+    return count - 1
+
+
+def gather(proj_ref, sig_ref, proj_out, sig_out, proj_send, proj_recv, sig_send, sig_recv):
     count, me = lax.axis_size("freq"), lax.axis_index("freq")
-    barrier, peers = greet("freq")
+    barrier = pltpu.get_barrier_semaphore()
+    peers = greet(barrier, "freq") + greet(barrier, "kpt")
     points, rows, bands = proj_ref.shape
     padded = proj_out.shape[2]
     own = proj_ref[...]
@@ -371,32 +354,9 @@
         copy.wait_send()
 
 
-def gather(proj, sig, count):
-    points, rows, bands = proj.shape
-    padded = -(-rows // 16) * 16
-    vmem = pl.BlockSpec(memory_space=pltpu.VMEM)
-    return pl.pallas_call(
-        gather_kernel,
-        out_shape=(
-            jax.ShapeDtypeStruct((count, points, padded, bands), proj.dtype),
-            jax.ShapeDtypeStruct(sig.shape, sig.dtype),
-        ),
-        in_specs=[vmem, vmem],
-        out_specs=(vmem, vmem),
-        scratch_shapes=[pltpu.SemaphoreType.DMA((count,))] * 4,
-        compiler_params=pltpu.CompilerParams(
-            collective_id=0, has_side_effects=True, vmem_limit_bytes=32 * 1024 * 1024
-        ),
-        name="gather",
-    )(proj, sig)
-
-
-def exchange_kernel(mine_ref, out_ref, theirs, summed, kpt_sems, freq_send, freq_recv):
+def exchange(mine_ref, out_ref, theirs, summed, kpt_sems, freq_send, freq_recv):
     count, me = lax.axis_size("freq"), lax.axis_index("freq")
     others, point = lax.axis_size("kpt"), lax.axis_index("kpt")
-    _, peers = greet("freq")
-    barrier, more = greet("kpt")
-    pl.semaphore_wait(barrier, peers + more)
     kpt_send, kpt_recv = kpt_sems.at[0], kpt_sems.at[1]
     copies = []
     for j in range(1, others):
@@ -446,51 +406,63 @@
         copy.wait_send()
 
 
-def exchange(blocks, count, others):
-    atoms, kinds = blocks.shape
-    each = atoms // (count * others)
-    vmem = pl.BlockSpec(memory_space=pltpu.VMEM)
-    return pl.pallas_call(
-        exchange_kernel,
-        out_shape=jax.ShapeDtypeStruct((count, each, kinds), blocks.dtype),
-        in_specs=[vmem],
-        out_specs=vmem,
-        scratch_shapes=[
-            pltpu.VMEM((others, atoms // others, kinds), blocks.dtype),
-            pltpu.VMEM((count, each, kinds), blocks.dtype),
-            pltpu.SemaphoreType.DMA((2, others)),
-            pltpu.SemaphoreType.DMA((count,)),
-            pltpu.SemaphoreType.DMA((count,)),
-        ],
-        compiler_params=pltpu.CompilerParams(collective_id=1, has_side_effects=True),
-        name="exchange",
-    )(blocks.reshape(others, atoms // others, kinds))
+def whole_kernel(
+    points, kweight, proj_ref, sig_ref, slot_ref, back_ref, energy_ref, out_ref,
+    proj_all, sig_all, mine, theirs, summed, mr, mi, pm, gather_sems, kpt_sems, end_sems,
+):
+    gather(proj_ref, sig_ref, proj_all, sig_all, *(gather_sems.at[i] for i in range(4)))
+    value = None
+    for point in range(points):
+        block = point_blocks(
+            point, points, kweight, proj_all[:, point], sig_all, slot_ref, back_ref, energy_ref, mr, mi, pm
+        )
+        value = block if value is None else value + block
+    share = mine.shape[1]
+    for part in range(mine.shape[0]):
+        mine[part] = value[part * share : (part + 1) * share]
+    exchange(mine, out_ref, theirs, summed, kpt_sems, end_sems.at[0], end_sems.at[1])
 
 
 def local(band_energy, projector, sigma, atom_of_slot, kweight):
     count, others = lax.axis_size("freq"), lax.axis_size("kpt")
-    points = band_energy.shape[0]
+    points, rows, bands = projector.shape
     atoms = atom_of_slot.shape[0]
     kinds = 2 * ORBS * ORBS
     slots = sigma.shape[3]
+    extra = -slots % 8
     sig = jnp.transpose(sigma.reshape(kinds, slots, count), (2, 1, 0))
-    projections, sig = gather(projector, sig, count)
-    sig = sig.reshape(atoms, kinds)
+    held = atom_of_slot.reshape(count, slots)
+    if extra:
+        sig = jnp.pad(sig, ((0, 0), (0, extra), (0, 0)))
+        held = jnp.pad(held, ((0, 0), (0, extra)), constant_values=-1)
     order = atom_of_slot.reshape(count, others, -1).transpose(1, 0, 2).reshape(1, atoms)
-    summed = None
-    for point in range(points):
-        block = point_blocks(
-            point,
-            points,
-            kweight,
-            projections[:, point],
-            sig,
-            atom_of_slot.reshape(1, atoms),
-            order,
-            band_energy[point : point + 1],
-        )
-        summed = block if summed is None else summed + block
-    owned = exchange(summed, count, others)
+    each = atoms // (count * others)
+    padded = -(-rows // 16) * 16
+    f32 = jnp.float32
+    vmem = pl.BlockSpec(memory_space=pltpu.VMEM)
+    owned = pl.pallas_call(
+        functools.partial(whole_kernel, points),
+        out_shape=jax.ShapeDtypeStruct((count, each, kinds), f32),
+        in_specs=[pl.BlockSpec(memory_space=pltpu.SMEM)] + [vmem] * 5,
+        out_specs=vmem,
+        scratch_shapes=[
+            pltpu.VMEM((count, points, padded, bands), projector.dtype),
+            pltpu.VMEM(sig.shape, f32),
+            pltpu.VMEM((others, atoms // others, kinds), f32),
+            pltpu.VMEM((others, atoms // others, kinds), f32),
+            pltpu.VMEM((count, each, kinds), f32),
+            pltpu.VMEM((bands, bands), f32),
+            pltpu.VMEM((bands, bands), f32),
+            pltpu.VMEM((ORBS * atoms, bands), jnp.bfloat16),
+            pltpu.SemaphoreType.DMA((4, count)),
+            pltpu.SemaphoreType.DMA((2, others)),
+            pltpu.SemaphoreType.DMA((2, count)),
+        ],
+        compiler_params=pltpu.CompilerParams(
+            collective_id=0, has_side_effects=True, vmem_limit_bytes=56 * 1024 * 1024
+        ),
+        name="whole",
+    )(kweight, projector, sig, held.reshape(1, -1), order, band_energy)
     return jnp.transpose(owned, (2, 1, 0)).reshape(2, ORBS, ORBS, -1, count)
 
 

time: 71.1 us -> 67.3 us (0.947)
  Pallas kernels: 65.4 us -> 62.4 us
  local copies, waits for them, and re-layouts: 5.42 us -> 4.65 us
    pallas_call x3 -> x1, Pallas kernels: 65.4 us -> 62.4 us  [local(): pl.pallas_call(functools.partial(whole_kernel, points), out_shape=jax.Sha...]
    unnamed x8 -> x2, local copies, waits for them, and re-layouts: 2.11 us -> 0.65 us
where the time goes in v3:
time: 67.3 us; the launch traced here: 67.1 us
  Pallas kernels  62.4 us (93%)
  local copies, waits for them, and re-layouts  4.65 us (7%)
    pallas_call x1, Pallas kernels, local(): pl.pallas_call(functools.partial(whole_kernel, points), out_shape=jax.Sha...  62.4 us
    reshape x1, local copies, waits for them, and re-layouts, local(): sig = jnp.transpose(sigma.reshape(kinds, slots, count), (2, 1, 0))  1.69 us
    transpose x1, local copies, waits for them, and re-layouts, local(): return jnp.transpose(owned, (2, 1, 0)).reshape(2, ORBS, ORBS, -1, count)  1.51 us

profile of v3, /device:TPU:0, one launch (start us, length us, event | category | flops | bytes accessed | tf_op | source)
XLA Modules:
  0.0 67.1 jit_solution(5668227979726778626)
XLA Ops:
  0.0 0.0 copy-start
  0.0 0.7 copy-done
  0.7 0.1 reshape.13
  0.8 0.7 %reshape.14.back_ref = s32[1,128]{1,0:T(1,128)} reshape(s32[2,16,4]{2,1,0:T(8,128)S(1)} %copy.10) | data formatting | bytes 1024 | tf_op jit(solution)/shard_map/reshape | solution.py:438
  1.5 1.7 %copy.9 = f32[50,8,16]{0,1,2:T(8,128)} copy(f32[50,8,16]{2,1,0:T(8,128)} %bitcast.7) | data formatting | bytes 51200 | tf_op jit(solution)/shard_map/reshape | solution.py:433
  3.2 62.4 %whole.1 = f32[16,4,50]{2,1,0:T(4,128)} custom-call(s32[2]{0:T(128)} %kweight.1, bf16[1,40,384]{2,1,0:T(8,128)(2,1)} %proj_ref.1, f32[16,8,50]{2,1,0:T(8,128)} %bitcast.6, s32[1,128]{1,0:T(1,128)} %bitcast.10, s32[1,128]{1,0:T(1,128)} %reshape.14.back_ref, f32[1,384]{1,0:T(1,128)} %energy_ref.1), custom_call_target="tpu_custom_call" | custom-call | tf_op jit(solution)/shard_map/whole/pallas_call | solution.py:443
  65.6 1.5 %copy.11 = f32[50,4,16]{2,1,0:T(4,128)} copy(f32[50,4,16]{0,1,2:T(4,128)} %bitcast.8) | data formatting | bytes 25600 | tf_op jit(solution)/shard_map/transpose | solution.py:466
  (1 shorter events, 0.0 us)
Async XLA Ops:
  0.0 0.7 copy-start

commit v4 on v3

--- a/solution.py
+++ b/solution.py
@@ -11,7 +11,7 @@
 ORBS = 5
 TILE = 128
 MESH = pl.DeviceIdType.MESH
-STEP = 32
+STEP = 64
 
 HIGH = lax.Precision.HIGHEST
 BETA_INV = 0.1
@@ -268,19 +268,25 @@
     return made
 
 
-def greet(barrier, axis):
-    count, me = lax.axis_size(axis), lax.axis_index(axis)
-    for j in range(1, count):
-        pl.semaphore_signal(
-            barrier, inc=1, device_id={axis: lax.rem(me + j, count)}, device_id_type=MESH
-        )
-    return count - 1
+def others_of():
+    count, me = lax.axis_size("freq"), lax.axis_index("freq")
+    points, point = lax.axis_size("kpt"), lax.axis_index("kpt")
+    return [
+        (lax.rem(me + j, count), lax.rem(point + p, points))
+        for j in range(count)
+        for p in range(points)
+        if j + p > 0
+    ]
 
 
 def gather(proj_ref, sig_ref, proj_out, sig_out, proj_send, proj_recv, sig_send, sig_recv):
     count, me = lax.axis_size("freq"), lax.axis_index("freq")
     barrier = pltpu.get_barrier_semaphore()
-    peers = greet(barrier, "freq") + greet(barrier, "kpt")
+    peers = others_of()
+    for freq, kpt in peers:
+        pl.semaphore_signal(
+            barrier, inc=1, device_id={"freq": freq, "kpt": kpt}, device_id_type=MESH
+        )
     points, rows, bands = proj_ref.shape
     padded = proj_out.shape[2]
     own = proj_ref[...]
@@ -288,7 +294,7 @@
         own = jnp.concatenate([own, jnp.zeros((points, padded - rows, bands), own.dtype)], axis=1)
     proj_out[me] = own
     sig_out[me] = sig_ref[me]
-    pl.semaphore_wait(barrier, peers)
+    pl.semaphore_wait(barrier, len(peers))
 
     dims = radices(count)
     strides = [math.prod(dims[s + 1 :]) for s in range(len(dims))]
@@ -354,61 +360,37 @@
         copy.wait_send()
 
 
-def exchange(mine_ref, out_ref, theirs, summed, kpt_sems, freq_send, freq_recv):
-    count, me = lax.axis_size("freq"), lax.axis_index("freq")
-    others, point = lax.axis_size("kpt"), lax.axis_index("kpt")
-    kpt_send, kpt_recv = kpt_sems.at[0], kpt_sems.at[1]
-    copies = []
-    for j in range(1, others):
-        target = lax.rem(point + j, others)
-        copy = pltpu.make_async_remote_copy(
-            src_ref=mine_ref.at[target],
-            dst_ref=theirs.at[j],
-            send_sem=kpt_send.at[j],
-            recv_sem=kpt_recv.at[j],
-            device_id={"kpt": target},
+def exchange(mine, landed, out_ref, sends, recvs):
+    me, point = lax.axis_index("freq"), lax.axis_index("kpt")
+
+    def part(freq, kpt, to_freq, to_kpt):
+        return pltpu.make_async_remote_copy(
+            src_ref=mine.at[to_kpt, to_freq],
+            dst_ref=landed.at[kpt, freq],
+            send_sem=sends.at[to_kpt, to_freq],
+            recv_sem=recvs.at[kpt, freq],
+            device_id={"freq": to_freq, "kpt": to_kpt},
             device_id_type=MESH,
         )
+
+    peers = others_of()
+    copies = [part(me, point, *peer) for peer in peers]
+    for copy in copies:
         copy.start()
-        copies.append(copy)
-    total = mine_ref[point]
-    for j in range(1, others):
-        copies[j - 1].wait()
-        total = total + theirs[j]
-    each = summed.shape[1]
-    for owner in range(count):
-        summed[owner] = total[owner * each : (owner + 1) * each]
-    copies = []
-    for j in range(1, count):
-        target = lax.rem(me + j, count)
-        copy = pltpu.make_async_remote_copy(
-            src_ref=summed.at[target],
-            dst_ref=out_ref.at[me],
-            send_sem=freq_send.at[j],
-            recv_sem=freq_recv.at[me],
-            device_id={"freq": target},
-            device_id_type=MESH,
-        )
-        copy.start()
-        copies.append(copy)
-    out_ref[me] = summed[me]
-    for j in range(1, count):
-        source = lax.rem(me + j, count)
-        pltpu.make_async_remote_copy(
-            src_ref=summed.at[source],
-            dst_ref=out_ref.at[source],
-            send_sem=freq_send.at[j],
-            recv_sem=freq_recv.at[source],
-            device_id={"freq": source},
-            device_id_type=MESH,
-        ).wait_recv()
+    landed[point, me] = mine[point, me]
+    for freq, kpt in peers:
+        part(freq, kpt, freq, kpt).wait_recv()
+    total = landed[0]
+    for kpt in range(1, landed.shape[0]):
+        total = total + landed[kpt]
+    out_ref[...] = total
     for copy in copies:
         copy.wait_send()
 
 
 def whole_kernel(
     points, kweight, proj_ref, sig_ref, slot_ref, back_ref, energy_ref, out_ref,
-    proj_all, sig_all, mine, theirs, summed, mr, mi, pm, gather_sems, kpt_sems, end_sems,
+    proj_all, sig_all, mine, landed, mr, mi, pm, gather_sems, end_sems,
 ):
     gather(proj_ref, sig_ref, proj_all, sig_all, *(gather_sems.at[i] for i in range(4)))
     value = None
@@ -417,10 +399,12 @@
             point, points, kweight, proj_all[:, point], sig_all, slot_ref, back_ref, energy_ref, mr, mi, pm
         )
         value = block if value is None else value + block
-    share = mine.shape[1]
-    for part in range(mine.shape[0]):
-        mine[part] = value[part * share : (part + 1) * share]
-    exchange(mine, out_ref, theirs, summed, kpt_sems, end_sems.at[0], end_sems.at[1])
+    parts, owners, each, _ = mine.shape
+    for part in range(parts):
+        for owner in range(owners):
+            first = (part * owners + owner) * each
+            mine[part, owner] = value[first : first + each]
+    exchange(mine, landed, out_ref, end_sems.at[0], end_sems.at[1])
 
 
 def local(band_energy, projector, sigma, atom_of_slot, kweight):
@@ -448,15 +432,13 @@
         scratch_shapes=[
             pltpu.VMEM((count, points, padded, bands), projector.dtype),
             pltpu.VMEM(sig.shape, f32),
-            pltpu.VMEM((others, atoms // others, kinds), f32),
-            pltpu.VMEM((others, atoms // others, kinds), f32),
-            pltpu.VMEM((count, each, kinds), f32),
+            pltpu.VMEM((others, count, each, kinds), f32),
+            pltpu.VMEM((others, count, each, kinds), f32),
             pltpu.VMEM((bands, bands), f32),
             pltpu.VMEM((bands, bands), f32),
             pltpu.VMEM((ORBS * atoms, bands), jnp.bfloat16),
             pltpu.SemaphoreType.DMA((4, count)),
-            pltpu.SemaphoreType.DMA((2, others)),
-            pltpu.SemaphoreType.DMA((2, count)),
+            pltpu.SemaphoreType.DMA((2, others, count)),
         ],
         compiler_params=pltpu.CompilerParams(
             collective_id=0, has_side_effects=True, vmem_limit_bytes=56 * 1024 * 1024

time: 67.3 us -> 69.2 us (1.028)
  Pallas kernels: 62.4 us -> 64.3 us
    pallas_call x1, Pallas kernels: 62.4 us -> 64.3 us  [local(): pl.pallas_call(functools.partial(whole_kernel, points), out_shape=jax.Sha...]
where the time goes in v4:
time: 69.2 us; the launch traced here: 68.9 us
  Pallas kernels  64.3 us (93%)
  local copies, waits for them, and re-layouts  4.65 us (7%)
    pallas_call x1, Pallas kernels, local(): pl.pallas_call(functools.partial(whole_kernel, points), out_shape=jax.Sha...  64.3 us
    reshape x1, local copies, waits for them, and re-layouts, local(): sig = jnp.transpose(sigma.reshape(kinds, slots, count), (2, 1, 0))  1.69 us
    transpose x1, local copies, waits for them, and re-layouts, local(): return jnp.transpose(owned, (2, 1, 0)).reshape(2, ORBS, ORBS, -1, count)  1.51 us

profile of v4, /device:TPU:0, one launch (start us, length us, event | category | flops | bytes accessed | tf_op | source)
XLA Modules:
  0.0 68.9 jit_solution(2972728655220143252)
XLA Ops:
  0.0 0.0 copy-start
  0.0 0.7 copy-done
  0.7 0.1 reshape.13
  0.8 0.7 reshape.14.back_ref
  1.5 1.7 %copy.9 = f32[50,8,16]{0,1,2:T(8,128)} copy(f32[50,8,16]{2,1,0:T(8,128)} %bitcast.7) | data formatting | bytes 51200 | tf_op jit(solution)/shard_map/reshape | solution.py:417
  3.2 64.3 %whole.1 = f32[16,4,50]{2,1,0:T(4,128)} custom-call(s32[2]{0:T(128)} %kweight.1, bf16[1,40,384]{2,1,0:T(8,128)(2,1)} %proj_ref.1, f32[16,8,50]{2,1,0:T(8,128)} %bitcast.6, s32[1,128]{1,0:T(1,128)} %bitcast.10, s32[1,128]{1,0:T(1,128)} %reshape.14.back_ref, f32[1,384]{1,0:T(1,128)} %energy_ref.1), custom_call_target="tpu_custom_call" | custom-call | tf_op jit(solution)/shard_map/whole/pallas_call | solution.py:427
  67.4 1.5 %copy.11 = f32[50,4,16]{2,1,0:T(4,128)} copy(f32[50,4,16]{0,1,2:T(4,128)} %bitcast.8) | data formatting | bytes 25600 | tf_op jit(solution)/shard_map/transpose | solution.py:448
  (1 shorter events, 0.0 us)
Async XLA Ops:
  0.0 0.7 copy-start
